TPU v7x, 32 devices: a whole 2x2x4 slice. The times are simulated.
32 devices in a mesh: member: 2 (over x), lon: 16 (over z, y, core).
Axes of the slice: x: 2, y: 2, z: 4, core: 2. Of those that a mesh axis runs over, the one named last changes fastest.
Arguments:
- tracer_field: float32 [16, 2, 192, 768], P('member', None, 'lon'), parts along dimension 0, may hold values from -6 to 6
- courant_lon: float32 [4, 192, 768], P('member', 'lon'), parts along dimension 0, may hold values from -0.4 to 0.4
- courant_lat: float32 [4, 192, 768], P('member', 'lon'), parts along dimension 0, may hold values from -0.4 to 0.4
- diffusivity: float32 [2, 192, 768], P('member', 'lon'), parts along dimension 0, may hold values from 0.1 to 4
- polar_mask: int32 [768], replicated, may hold values from 0 to 1, as said below
- cutoff: int32 [768], replicated, may hold values from 4 to 95, as said below
Outputs:
- updated_field: float32 [16, 2, 192, 768], P('member', None, 'lon'), parts along dimension 0
There are 2 independent parts, one for each index of `member`. A program takes and returns all parts, laid end to end along the dimension named above; an argument that names none is the same for every part. Nothing has to cross between parts.
Inputs may be any that keep to these rules, and one draw needn't show every extreme that they name: `polar_mask`: 1 on the first 128 rows and on a last run of 64 to 128 rows, 0 elsewhere. `cutoff`: only rows with mask 1 use it.
All inputs are finite; a program needn't handle non-finite values.
Results may differ from a plain program's by a relative error of at most 0.00005.
Values sent between devices are 32-bit elements; how exact they have to be, the bound alone decides.
A program may use at most 128 MiB of HBM per device.

v0:
```python
import math

import jax
import jax.numpy as jnp
from jax import lax
from jax.sharding import PartitionSpec as P


def padded(x, sides, width):
    for axis, dim in sides:
        size, length = (lax.axis_size(axis), x.shape[dim])
        up = [(i, (i + 1) % size) for i in range(size)]
        down = [(j, i) for i, j in up]
        last = lax.slice_in_dim(x, length - width, length, axis=dim)
        leading = lax.slice_in_dim(x, 0, width, axis=dim)
        before = lax.ppermute(last, axis, up)
        after = lax.ppermute(leading, axis, down)
        x = jnp.concatenate([before, x, after], axis=dim)
    return x


def vertical_solve(diffusivity, field):
    levels = field.shape[1]
    zeros_plane = jnp.zeros_like(diffusivity[0])
    upper_list = []
    rhs_list = []
    prev_upper = None
    prev_rhs = None
    for lev_index in range(levels):
        below = diffusivity[lev_index - 1] if lev_index > 0 else zeros_plane
        above = diffusivity[lev_index] if lev_index < levels - 1 else zeros_plane
        diagonal = 1.0 + below + above
        source = field[:, lev_index]
        if lev_index == 0:
            denom = diagonal
            new_rhs = source / denom
        else:
            denom = diagonal + below * prev_upper
            new_rhs = (source + below * prev_rhs) / denom
        new_upper = -above / denom
        upper_list.append(new_upper)
        rhs_list.append(new_rhs)
        prev_upper = new_upper
        prev_rhs = new_rhs
    result = [None] * levels
    current = rhs_list[levels - 1]
    result[levels - 1] = current
    lev_index = 0
    current = rhs_list[lev_index] - upper_list[lev_index] * current
    result[lev_index] = current
    return jnp.stack(result, axis=1)


def fourier_tables(length):
    half_len = length // 2
    column = jnp.arange(length, dtype=jnp.int32)[:, None]
    wavenum = jnp.arange(1, half_len + 1, dtype=jnp.int32)[None, :]
    phase = column * wavenum % length
    angle = 2.0 * math.pi / length * phase.astype(jnp.float32)
    return (jnp.cos(angle), jnp.sin(angle))


def high_part(block, row_cut, cosine, sine):
    length = block.shape[1]
    half_len = length // 2
    highest = lax.Precision.HIGHEST
    real_part = jnp.einsum("bir,im->brm", block, cosine, precision=highest)
    imag_part = jnp.einsum("bir,im->brm", block, sine, precision=highest)
    wavenum = jnp.arange(1, half_len + 1, dtype=jnp.int32)
    weights = jnp.where(wavenum == half_len, 1.0 / length, 2.0 / length).astype(jnp.float32)
    keeper = jnp.where(wavenum[None, :] > row_cut[:, None], weights[None, :], 0.0)
    return jnp.einsum(
        "brm,im->bir", real_part * keeper[None], cosine, precision=highest
    ) + jnp.einsum("brm,im->bir", imag_part * keeper[None], sine, precision=highest)


def local(tracer_field, courant_lon, courant_lat, diffusivity, polar_mask, cutoff):
    tracers, levels, lon_local, lat_rows = tracer_field.shape
    zero_row = jnp.zeros_like(tracer_field[..., :1])
    north_next = jnp.concatenate([tracer_field[..., 1:], zero_row], axis=3)
    north = (
        jnp.maximum(courant_lat, 0.0)[None] * tracer_field
        + jnp.minimum(courant_lat, 0.0)[None] * north_next
    )
    south = jnp.concatenate([zero_row, north[..., :-1]], axis=3)
    stacked = jnp.concatenate([tracer_field, courant_lon[None]], axis=0)
    extended = padded(stacked, (("lon", 2),), 1)
    tracer_ext = extended[:tracers]
    speed_ext = extended[tracers][None, :, :-1]
    east_all = (
        jnp.maximum(speed_ext, 0.0) * tracer_ext[:, :, :-1]
        + jnp.minimum(speed_ext, 0.0) * tracer_ext[:, :, 1:]
    )
    east = east_all[:, :, 1:]
    west = east_all[:, :, :-1]
    advected = tracer_field - (east - west) - (north - south)
    batched = advected.reshape(tracers * levels, lon_local, lat_rows)
    length = lon_local * lax.axis_size("lon")
    cosine, sine = fourier_tables(length)
    mask_float = polar_mask.astype(jnp.float32)
    row_count = lat_rows // lax.axis_size("lon")
    first_row = lax.axis_index("lon") * row_count
    my_cut = lax.dynamic_slice_in_dim(cutoff, first_row, row_count)
    my_mask = lax.dynamic_slice_in_dim(mask_float, first_row, row_count)
    removed = (
        high_part(
            lax.all_to_all(batched, "lon", split_axis=2, concat_axis=1, tiled=True),
            my_cut,
            cosine,
            sine,
        )
        * my_mask[None, None, :]
    )
    correction = lax.all_to_all(removed, "lon", split_axis=1, concat_axis=2, tiled=True)
    filtered = (batched - correction).reshape(tracers, levels, lon_local, lat_rows)
    return vertical_solve(diffusivity, filtered)


def solution(mesh):
    placed = (
        P("member", None, "lon", None),
        P("member", "lon", None),
        P("member", "lon", None),
        P("member", "lon", None),
        P(),
        P(),
    )
    return jax.shard_map(
        local, mesh=mesh, in_specs=placed, out_specs=P("member", None, "lon", None), check_vma=False
    )
```

profile of v0, /device:TPU:0, one launch (start us, length us, event | category | flops | bytes accessed | tf_op | source)
XLA Modules:
  0.0 89.5 jit_solution(6929786615368778992)
XLA Ops:
  0.0 1.0 %pad_maximum_fusion.9 = (f32[9,2,1,768]{3,1,0,2:T(2,128)S(1)}, f32[9,2,1,768]{3,1,0,2:T(2,128)S(1)}) fusion(f32[1,2,12,768]{3,1,0,2:T(2,128)} %bitcast.52, f32[8,2,12,768]{3,1,2,0:T(2,128)} %param.6), kind=kLoop, calls=%fused_computation.42 | loop fusion | flops 27648 | bytes 774144 | tf_op jit(solution)/shard_map/slice | solution.py:14
  1.0 0.5 collective-permute-start
  1.5 5.1 %collective-permute-start.1 = (f32[9,2,1,768]{3,1,0,2:T(2,128)S(1)}, f32[9,2,1,768]{3,1,0,2:T(2,128)S(1)}, u32[]{:S(2)}, u32[]{:S(2)}) collective-permute-start(f32[9,2,1,768]{3,1,0,2:T(2,128)S(1)} %get-tuple-element.10), channel_id=1, source_target_pairs={{1,0},{2,1},{3,2},{4,3},{5,4},{6,5},{7,6},{8,7},{9,8},{10,9},{11,1... | collective-permute-start | bytes 165896 | tf_op jit(solution)/shard_map/ppermute | solution.py:17
  6.5 1.7 %slice.56 = f32[8,2,12,767]{3,1,2,0:T(2,128)S(1)} slice(f32[8,2,12,768]{3,1,2,0:T(2,128)} %param.6), slice={[0:8], [0:2], [0:12], [1:768]} | slice | bytes 1178112 | tf_op jit(solution)/shard_map/slice | solution.py:80
  8.5 0.4 multiply_add_fusion
  9.8 0.8 fusion.6
  10.6 0.4 reshape.61
  11.0 5.0 %copy.19 = f32[16,12,768]{0,1,2:T(8,128)} copy(f32[16,12,768]{2,0,1:T(8,128)S(1)} %reshape.61) | data formatting | bytes 1179648 | tf_op jit(solution)/shard_map/reshape | solution.py:97
  16.0 5.5 %reshape.64 = f32[16,1,9216]{2,1,0:T(1,128)} reshape(f32[768,12,16]{2,1,0:T(8,128)} %bitcast.46) | data formatting | bytes 1179648
  21.4 5.0 %all-to-all-start = ((f32[16,1,9216]{2,1,0:T(1,128)}), f32[16,1,9216]{2,1,0:T(1,128)S(1)}, u32[]{:S(2)}, u32[]{:S(2)}) async-start(f32[16,1,9216]{2,1,0:T(1,128)} %reshape.64), calls=%async_computation | async-start | bytes 1179648 | tf_op jit(solution)/shard_map/all_to_all | solution.py:107
  26.4 0.8 dynamic_slice.6
  27.4 14.6 %all-to-all-done = f32[16,1,9216]{2,1,0:T(1,128)S(1)} async-done(((f32[16,1,9216]{2,1,0:T(1,128)}), f32[16,1,9216]{2,1,0:T(1,128)S(1)}, u32[]{:S(2)}, u32[]{:S(2)}) %all-to-all-start) | async-done | bytes 589856 | tf_op jit(solution)/shard_map/all_to_all | solution.py:107
  42.0 0.5 broadcast.105
  42.5 1.9 %reduce = f32[16,9216]{1,0:T(8,128)S(1)} reduce(f32[16,1,9216]{2,1,0:T(1,128)S(1)} %all-to-all-done, f32[]{:T(128)} %broadcast.105), dimensions={1}, to_apply=%all_to_all.26.reduce_sub_computation | reduce | bytes 1179652 | tf_op jit(solution)/shard_map/all_to_all | solution.py:107
  44.4 4.4 %reshape.65 = f32[768,12,16]{2,1,0:T(8,128)} reshape(f32[16,9216]{1,0:T(8,128)S(1)} %reduce) | data formatting | bytes 1179648
  48.8 4.7 %copy.21 = f32[16,16,12,48]{3,0,2,1:T(8,128)S(1)} copy(f32[16,16,12,48]{0,2,3,1:T(8,128)} %bitcast.47) | data formatting | bytes 1179648 | tf_op jit(solution)/shard_map/all_to_all | solution.py:107
  53.5 0.8 copy.22
  54.3 1.2 %convolution_multiply_fusion.1 = f32[16,48,96]{2,1,0:T(8,128)S(1)} fusion(f32[16,192,48]{1,2,0:T(8,128)S(1)} %copy.22, f32[48,96]{1,0:T(8,128)S(1)} %compare_select_fusion, s32[96]{0:T(128)S(1)} %iota_add_fusion), kind=kOutput, calls=%fused_computation.4 | convolution fusion | flops 170108928 | bytes 903552 | tf_op jit(solution)/shard_map/bir,im->brm/dot_general | solution.py:67
  55.4 1.2 %convolution_multiply_fusion = f32[16,48,96]{2,1,0:T(8,128)S(1)} fusion(f32[16,192,48]{1,2,0:T(8,128)S(1)} %copy.22, f32[48,96]{1,0:T(8,128)S(1)} %compare_select_fusion, s32[96]{0:T(128)S(1)} %iota_add_fusion), kind=kOutput, calls=%fused_computation.3 | convolution fusion | flops 170108928 | bytes 903552 | tf_op jit(solution)/shard_map/bir,im->brm/dot_general | solution.py:68
  56.6 1.2 %fusion.12 = f32[192,16,48]{0,2,1:T(8,128)S(1)} fusion(f32[16,48,96]{2,1,0:T(8,128)S(1)} %convolution_multiply_fusion.1, s32[96]{0:T(128)S(1)} %iota_add_fusion), kind=kOutput, calls=%fused_computation.26 | convolution fusion | flops 170035200 | bytes 885120 | tf_op jit(solution)/shard_map/brm,im->bir/dot_general | solution.py:72
  57.8 1.2 %fusion.1 = f32[16,192,48]{1,2,0:T(8,128)S(1)} fusion(f32[192,16,48]{0,2,1:T(8,128)S(1)} %fusion.12, f32[16,48,96]{2,1,0:T(8,128)S(1)} %convolution_multiply_fusion, f32[48]{0:T(128)S(1)} %dynamic_slice.7, s32[96]{0:T(128)S(1)} %iota_add_fusion), kind=kOutput, calls=%fused_computation.2 | convolution fusion | flops 170330112 | bytes 1475136 | tf_op jit(solution)/shard_map/brm,im->bir/dot_general | solution.py:74
  58.9 0.8 copy.24
  59.8 2.4 %reshape.66 = f32[16,1,9216]{2,1,0:T(1,128)} reshape(f32[192,16,48]{2,1,0:T(8,128)S(1)} %bitcast.48) | data formatting | bytes 1179648
  62.2 4.4 %all-to-all-start.1 = ((f32[16,1,9216]{2,1,0:T(1,128)}), f32[16,1,9216]{2,1,0:T(1,128)S(1)}, u32[]{:S(2)}, u32[]{:S(2)}) async-start(f32[16,1,9216]{2,1,0:T(1,128)} %reshape.66), calls=%async_computation.1 | async-start | bytes 1179648 | tf_op jit(solution)/shard_map/all_to_all | solution.py:114
  66.7 15.4 %all-to-all-done.1 = f32[16,1,9216]{2,1,0:T(1,128)S(1)} async-done(((f32[16,1,9216]{2,1,0:T(1,128)}), f32[16,1,9216]{2,1,0:T(1,128)S(1)}, u32[]{:S(2)}, u32[]{:S(2)}) %all-to-all-start.1) | async-done | bytes 589856 | tf_op jit(solution)/shard_map/all_to_all | solution.py:114
  82.2 2.0 %reduce.1 = f32[16,9216]{1,0:T(8,128)S(1)} reduce(f32[16,1,9216]{2,1,0:T(1,128)S(1)} %all-to-all-done.1, f32[]{:T(128)} %broadcast.105), dimensions={1}, to_apply=%all_to_all.30.reduce_sub_computation | reduce | bytes 1179652 | tf_op jit(solution)/shard_map/all_to_all | solution.py:114
  84.1 0.7 reshape.67
  84.8 0.9 %copy.25 = f32[16,12,16,48]{3,2,0,1:T(8,128)S(1)} copy(f32[16,12,16,48]{3,0,1,2:T(8,128)S(1)} %bitcast.49) | data formatting | bytes 1179648 | tf_op jit(solution)/shard_map/all_to_all | solution.py:114
  85.7 1.3 %all_to_all.33 = f32[8,2,12,768]{3,1,0,2:T(2,128)S(1)} reshape(f32[16,12,16,48]{3,2,0,1:T(8,128)S(1)} %copy.25) | data formatting | bytes 1179648 | tf_op jit(solution)/shard_map/all_to_all | solution.py:114
  87.4 0.7 multiply_subtract_fusion
  88.0 0.5 pad_maximum_fusion.4
  88.6 0.9 copy.26
  (30 shorter events, 1.6 us)
Async XLA Ops:
  0.0 8.3 %copy-start.5 = (f32[2,12,768]{2,0,1:T(2,128)S(1)}, f32[2,12,768]{2,0,1:T(2,128)}, u32[]{:S(2)}) copy-start(f32[2,12,768]{2,0,1:T(2,128)} %param.8) | copy-start | bytes 221188
  0.0 8.4 %copy-start = (f32[8,2,12,768]{3,1,2,0:T(2,128)S(1)}, f32[8,2,12,768]{3,1,2,0:T(2,128)}, u32[]{:S(2)}) copy-start(f32[8,2,12,768]{3,1,2,0:T(2,128)} %param.6) | copy-start | bytes 1769476
  1.0 7.9 %collective-permute-start = (f32[9,2,1,768]{3,1,0,2:T(2,128)S(1)}, f32[9,2,1,768]{3,1,0,2:T(2,128)S(1)}, u32[]{:S(2)}, u32[]{:S(2)}) collective-permute-start(f32[9,2,1,768]{3,1,0,2:T(2,128)S(1)} %get-tuple-element.9), channel_id=1, source_target_pairs={{0,1},{1,2},{2,3},{3,4},{4,5},{5,6},{6,7},{7,8},{8,9},{9,10},{10,1... | collective-permute-start | bytes 165896 | tf_op jit(solution)/shard_map/ppermute | solution.py:16
  1.5 7.4 %collective-permute-start.1 = (f32[9,2,1,768]{3,1,0,2:T(2,128)S(1)}, f32[9,2,1,768]{3,1,0,2:T(2,128)S(1)}, u32[]{:S(2)}, u32[]{:S(2)}) collective-permute-start(f32[9,2,1,768]{3,1,0,2:T(2,128)S(1)} %get-tuple-element.10), channel_id=1, source_target_pairs={{1,0},{2,1},{3,2},{4,3},{5,4},{6,5},{7,6},{8,7},{9,8},{10,9},{11,1... | collective-permute-start | bytes 165896 | tf_op jit(solution)/shard_map/ppermute | solution.py:17
  8.4 0.9 copy-start.3
  10.5 5.4 %copy-start.1 = (f32[8,2,12,768]{3,1,0,2:T(2,128)}, f32[8,2,12,768]{3,1,0,2:T(2,128)S(1)}, u32[]{:S(2)}) copy-start(f32[8,2,12,768]{3,1,0,2:T(2,128)S(1)} %fusion.6) | copy-start | bytes 1769476
  16.0 10.5 %copy-start.6 = (s32[768]{0:T(1024)S(1)}, s32[768]{0:T(1024)}, u32[]{:S(2)}) copy-start(s32[768]{0:T(1024)} %param.10) | copy-start | bytes 9220
  21.4 20.5 %all-to-all-start = ((f32[16,1,9216]{2,1,0:T(1,128)}), f32[16,1,9216]{2,1,0:T(1,128)S(1)}, u32[]{:S(2)}, u32[]{:S(2)}) async-start(f32[16,1,9216]{2,1,0:T(1,128)} %reshape.64), calls=%async_computation | async-start | bytes 1179648 | tf_op jit(solution)/shard_map/all_to_all | solution.py:107
  59.8 6.8 %copy-start.4 = (f32[1,12,768]{2,0,1:T(1,128)S(1)}, f32[1,12,768]{2,0,1:T(1,128)}, u32[]{:S(2)}) copy-start(f32[1,12,768]{2,0,1:T(1,128)} %param.9) | copy-start | bytes 110596
  62.2 20.0 %all-to-all-start.1 = ((f32[16,1,9216]{2,1,0:T(1,128)}), f32[16,1,9216]{2,1,0:T(1,128)S(1)}, u32[]{:S(2)}, u32[]{:S(2)}) async-start(f32[16,1,9216]{2,1,0:T(1,128)} %reshape.66), calls=%async_computation.1 | async-start | bytes 1179648 | tf_op jit(solution)/shard_map/all_to_all | solution.py:114
  85.7 1.3 %copy-start.2 = (f32[8,2,12,768]{3,1,0,2:T(2,128)S(1)}, f32[8,2,12,768]{3,1,0,2:T(2,128)}, u32[]{:S(2)}) copy-start(f32[8,2,12,768]{3,1,0,2:T(2,128)} %copy-done.1) | copy-start | bytes 1769476
where the time goes:
time: 90 us; the launch traced here: 89.5 us
  local copies, waits for them, and re-layouts  31.3 us (35%)
  waiting for transfers between devices  30 us (33%)
  starting transfers between devices  15 us (17%)
  other arithmetic  8.27 us (9%)
  matrix products  4.66 us (5%)
    all_to_all x1, waiting for transfers between devices, local(): lax.all_to_all(removed, 'lon', split_axis=1, concat_axis=2, tiled=True)  15.4 us
    all_to_all x1, waiting for transfers between devices, local(): lax.all_to_all(batched, 'lon', split_axis=2, concat_axis=1, tiled=True)  14.6 us
    unnamed x21, local copies, waits for them, and re-layouts  13.4 us
    all_to_all x3, local copies, waits for them, and re-layouts, local(): lax.all_to_all(batched, 'lon', split_axis=2, concat_axis=1, tiled=True)  5.92 us
    reshape x2, local copies, waits for them, and re-layouts, local(): batched = advected.reshape(tracers * levels, lon_local, lat_rows)  5.38 us
    ppermute x1, starting transfers between devices, padded(): after = lax.ppermute(leading, axis, down)  5.06 us
    all_to_all x1, starting transfers between devices, local(): lax.all_to_all(batched, 'lon', split_axis=2, concat_axis=1, tiled=True)  4.97 us
    all_to_all x1, starting transfers between devices, local(): lax.all_to_all(removed, 'lon', split_axis=1, concat_axis=2, tiled=True)  4.43 us
  transfers between devices with their start and end apart: 4, of which 2 were waited for; matrix products, arithmetic and copies ran while one was open for 4% of the time, Pallas kernels for 0%

commit v1 on v0

v1 whole, which is shorter than its diff:
```python
import functools
import math

import jax
import jax.numpy as jnp
import numpy as np
from jax import lax
from jax.experimental import pallas as pl
from jax.experimental.layout import Layout, with_layout_constraint
from jax.experimental.pallas import tpu as pltpu
from jax.sharding import PartitionSpec as P

POLAR = 128
LANES = 128


def padded(x, sides, width):
    for axis, dim in sides:
        size, length = (lax.axis_size(axis), x.shape[dim])
        up = [(i, (i + 1) % size) for i in range(size)]
        down = [(j, i) for i, j in up]
        last = lax.slice_in_dim(x, length - width, length, axis=dim)
        leading = lax.slice_in_dim(x, 0, width, axis=dim)
        before = lax.ppermute(last, axis, up)
        after = lax.ppermute(leading, axis, down)
        x = jnp.concatenate([before, x, after], axis=dim)
    return x


def fourier_tables(length):
    half_len = length // 2
    column = jnp.arange(length, dtype=jnp.int32)[:, None]
    wavenum = jnp.arange(1, half_len + 1, dtype=jnp.int32)[None, :]
    phase = column * wavenum % length
    angle = 2.0 * math.pi / length * phase.astype(jnp.float32)
    return (jnp.cos(angle), jnp.sin(angle))


def high_part(block, row_cut, cosine, sine):
    length = block.shape[1]
    half_len = length // 2
    highest = lax.Precision.HIGHEST
    real_part = jnp.einsum("bir,im->brm", block, cosine, precision=highest)
    imag_part = jnp.einsum("bir,im->brm", block, sine, precision=highest)
    wavenum = jnp.arange(1, half_len + 1, dtype=jnp.int32)
    weights = jnp.where(wavenum == half_len, 1.0 / length, 2.0 / length).astype(jnp.float32)
    keeper = jnp.where(wavenum[None, :] > row_cut[:, None], weights[None, :], 0.0)
    return jnp.einsum(
        "brm,im->bir", real_part * keeper[None], cosine, precision=highest
    ) + jnp.einsum("brm,im->bir", imag_part * keeper[None], sine, precision=highest)


def local_by_collectives(tracer_field, courant_lon, courant_lat, diffusivity, polar_mask, cutoff):
    tracers, levels, lon_local, lat_rows = tracer_field.shape
    zero_row = jnp.zeros_like(tracer_field[..., :1])
    north_next = jnp.concatenate([tracer_field[..., 1:], zero_row], axis=3)
    north = (
        jnp.maximum(courant_lat, 0.0)[None] * tracer_field
        + jnp.minimum(courant_lat, 0.0)[None] * north_next
    )
    south = jnp.concatenate([zero_row, north[..., :-1]], axis=3)
    stacked = jnp.concatenate([tracer_field, courant_lon[None]], axis=0)
    extended = padded(stacked, (("lon", 2),), 1)
    tracer_ext = extended[:tracers]
    speed_ext = extended[tracers][None, :, :-1]
    east_all = (
        jnp.maximum(speed_ext, 0.0) * tracer_ext[:, :, :-1]
        + jnp.minimum(speed_ext, 0.0) * tracer_ext[:, :, 1:]
    )
    advected = tracer_field - (east_all[:, :, 1:] - east_all[:, :, :-1]) - (north - south)
    batched = advected.reshape(tracers * levels, lon_local, lat_rows)
    ends = jnp.concatenate([batched[..., :POLAR], batched[..., lat_rows - POLAR :]], axis=2)
    ends_mask = jnp.concatenate([polar_mask[:POLAR], polar_mask[lat_rows - POLAR :]])
    ends_cut = jnp.concatenate([cutoff[:POLAR], cutoff[lat_rows - POLAR :]])
    size = lax.axis_size("lon")
    cosine, sine = fourier_tables(lon_local * size)
    row_count = 2 * POLAR // size
    first_row = lax.axis_index("lon") * row_count
    my_cut = lax.dynamic_slice_in_dim(ends_cut, first_row, row_count)
    my_mask = lax.dynamic_slice_in_dim(ends_mask.astype(jnp.float32), first_row, row_count)
    removed = (
        high_part(
            lax.all_to_all(ends, "lon", split_axis=2, concat_axis=1, tiled=True),
            my_cut,
            cosine,
            sine,
        )
        * my_mask[None, None, :]
    )
    correction = lax.all_to_all(removed, "lon", split_axis=1, concat_axis=2, tiled=True)
    filtered = jnp.concatenate(
        [
            batched[..., :POLAR] - correction[..., :POLAR],
            batched[..., POLAR : lat_rows - POLAR],
            batched[..., lat_rows - POLAR :] - correction[..., POLAR:],
        ],
        axis=2,
    ).reshape(tracers, levels, lon_local, lat_rows)
    share = diffusivity[0] / (1.0 + 2.0 * diffusivity[0])
    moved = share[None] * (filtered[:, 1] - filtered[:, 0])
    return jnp.stack([filtered[:, 0] + moved, filtered[:, 1] - moved], axis=1)


def orthonormal_rows(length):
    half = length // 2
    wave = np.arange(1, half + 1)[:, None]
    angle = 2.0 * np.pi / length * (wave * np.arange(length)[None, :] % length)
    scale = np.sqrt(np.where(wave == half, 1.0, 2.0) / length)
    return np.concatenate([np.cos(angle) * scale, np.sin(angle) * scale], axis=0)


def split(x):
    high = x.astype(jnp.bfloat16)
    return high, (x - high.astype(jnp.float32)).astype(jnp.bfloat16)


def product(a_high, a_low, b):
    b_high, b_low = split(b)
    dot = functools.partial(jnp.dot, preferred_element_type=jnp.float32)
    return dot(a_high, b_high) + (dot(a_high, b_low) + dot(a_low, b_high))


def kernel(
    n, tracers, lons, blocks,
    t_hbm, c_hbm, cl_hbm, kd_hbm, cut_hbm, mask_hbm, g_hbm, o_hbm,
    buf, clv, kv, cutv, maskv, gv, coef, adv, out_blocks, in_blocks, spec, back_blocks, corr,
    in_sem, halo_send, halo_recv, send_sem, recv_sem, back_send, back_recv, out_sem,
):
    rows = lons * blocks * 2
    stride = blocks * 2
    top = 16
    me = lax.axis_index("lon")
    right, left = lax.rem(me + 1, n), lax.rem(me + n - 1, n)
    my_pair = me // 2
    half = lax.rem(me, 2)

    loads = [
        pltpu.make_async_copy(c_hbm, buf.at[tracers, pl.ds(top, rows)], in_sem.at[0]),
        pltpu.make_async_copy(cl_hbm, clv.at[pl.ds(8, rows)], in_sem.at[1]),
        pltpu.make_async_copy(t_hbm, buf.at[pl.ds(0, tracers), pl.ds(top, rows)], in_sem.at[2]),
        pltpu.make_async_copy(kd_hbm, kv, in_sem.at[3]),
        pltpu.make_async_copy(cut_hbm, cutv, in_sem.at[4]),
        pltpu.make_async_copy(mask_hbm, maskv, in_sem.at[5]),
        pltpu.make_async_copy(g_hbm, gv, in_sem.at[6]),
    ]
    for load in loads:
        load.start()

    barrier = pltpu.get_barrier_semaphore()

    @pl.loop(1, n)
    def _(k):
        pl.semaphore_signal(barrier, inc=1, device_id={"lon": lax.rem(me + k, n)}, device_id_type=pl.DeviceIdType.MESH)

    pl.semaphore_wait(barrier, n - 1)

    def remote(src, dst, send, recv, to):
        return pltpu.make_async_remote_copy(
            src_ref=src, dst_ref=dst, send_sem=send, recv_sem=recv,
            device_id={"lon": to}, device_id_type=pl.DeviceIdType.MESH,
        )

    halos = [
        remote(c_hbm.at[pl.ds(rows - 16, 16)], buf.at[tracers, pl.ds(0, 16)], halo_send.at[0], halo_recv.at[0], right),
        remote(t_hbm.at[:, pl.ds(rows - 16, 16)], buf.at[pl.ds(0, tracers), pl.ds(0, 16)], halo_send.at[1], halo_recv.at[1], right),
        remote(t_hbm.at[:, pl.ds(0, 16)], buf.at[pl.ds(0, tracers), pl.ds(top + rows, 16)], halo_send.at[2], halo_recv.at[2], left),
    ]
    for halo in halos:
        halo.start()

    clv[pl.ds(0, 8)] = jnp.zeros((8, LANES), jnp.float32)
    loads[1].wait()
    row = lax.rem(lax.broadcasted_iota(jnp.int32, (rows, LANES), 0), stride)
    lane = lax.broadcasted_iota(jnp.int32, (rows, LANES), 1)
    last_lane, first_lane = lane == LANES - 1, lane == 0
    cl = clv[pl.ds(8, rows)]
    cl_prev = pltpu.roll(jnp.where(last_lane, clv[pl.ds(6, rows)], cl), 1, axis=1)
    cl_prev = jnp.where((row < 2) & first_lane, 0.0, cl_prev)
    north_next = jnp.where((row >= stride - 2) & last_lane, 0.0, jnp.minimum(cl, 0.0))
    coef[3] = -north_next
    coef[4] = jnp.maximum(cl_prev, 0.0)
    rest = 1.0 - jnp.maximum(cl, 0.0) + jnp.minimum(cl_prev, 0.0)
    loads[0].wait()
    halos[0].wait_recv()
    c = buf[tracers, pl.ds(top, rows)]
    c_west = buf[tracers, pl.ds(top - stride, rows)]
    coef[0] = rest - jnp.maximum(c, 0.0) + jnp.minimum(c_west, 0.0)
    coef[1] = -jnp.minimum(c, 0.0)
    coef[2] = jnp.maximum(c_west, 0.0)
    loads[2].wait()
    halos[1].wait_recv()
    halos[2].wait_recv()

    def send(dest):
        return remote(out_blocks.at[dest], in_blocks.at[me], send_sem.at[dest], recv_sem.at[me], dest)

    def advect(t):
        x = buf[t, pl.ds(top, rows)]
        y = jnp.where(first_lane, buf[t, pl.ds(top + 2, rows)], x)
        total = coef[0] * x + coef[3] * pltpu.roll(y, LANES - 1, axis=1)
        y = jnp.where(last_lane, buf[t, pl.ds(top - 2, rows)], x)
        total += coef[4] * pltpu.roll(y, 1, axis=1)
        total += coef[1] * buf[t, pl.ds(top + stride, rows)]
        total += coef[2] * buf[t, pl.ds(top - stride, rows)]
        adv[t] = total
        for h in range(2):
            for lev in range(2):
                first = h * (stride - 2) + lev
                out_blocks[2 * t + h, pl.ds(lev * lons, lons)] = adv[t, pl.ds(first, lons, stride=stride)]

    @pl.loop(1, tracers)
    def _(i):
        t = lax.rem(my_pair + i, tracers)
        advect(t)
        send(2 * t).start()
        send(2 * t + 1).start()

    advect(my_pair)
    twin = 2 * my_pair + 1 - half
    send(twin).start()
    in_blocks[me] = out_blocks[me]

    loads[3].wait()
    k = kv[...]
    kv[...] = k / (1.0 + 2.0 * k)

    def solve(t, block, remove):
        share = kv[pl.ds(block, lons, stride=blocks)]
        at = [pl.ds(2 * block + lev, lons, stride=stride) for lev in range(2)]
        upper, lower = adv[t, at[0]], adv[t, at[1]]
        if remove is not None:
            upper = upper - corr[remove, pl.ds(0, lons)]
            lower = lower - corr[remove, pl.ds(lons, lons)]
        moved = share * (lower - upper)
        adv[t, at[0]] = upper + moved
        adv[t, at[1]] = lower - moved

    @pl.loop(0, tracers)
    def _(t):
        for block in range(1, blocks - 1):
            solve(t, block, None)

    for load in loads[4:]:
        load.wait()

    def received(s):
        return remote(out_blocks.at[s], in_blocks.at[s], send_sem.at[s], recv_sem.at[s], s)

    @pl.loop(1, n)
    def _(k):
        received(lax.rem(me + n - k, n)).wait_recv()

    for s in range(n):
        for lev in range(2):
            spec[pl.ds(s * lons, lons), pl.ds(lev * LANES, LANES)] = in_blocks[s, pl.ds(lev * lons, lons)]

    length = n * lons
    cut = jnp.where(half == 0, cutv[pl.ds(0, LANES)], cutv[pl.ds((blocks - 1) * LANES, LANES)])
    mask = jnp.where(half == 0, maskv[pl.ds(0, LANES)], maskv[pl.ds((blocks - 1) * LANES, LANES)])
    cut = jnp.where(mask == 1, cut, length).reshape(1, LANES)
    wave = lax.rem(lax.broadcasted_iota(jnp.int32, (length, LANES), 0), length // 2) + 1
    keep = wave > cut
    waves = product(gv[0], gv[1], spec[...])
    waves = jnp.where(jnp.concatenate([keep, keep], axis=1), waves, 0.0)
    spec[...] = product(gv[2], gv[3], waves)
    for s in range(n):
        for lev in range(2):
            back_blocks[s, pl.ds(lev * lons, lons)] = spec[pl.ds(s * lons, lons), pl.ds(lev * LANES, LANES)]

    def back(dest):
        return remote(back_blocks.at[dest], corr.at[me], back_send.at[dest], back_recv.at[me], dest)

    @pl.loop(1, n)
    def _(k):
        back(lax.rem(me + k, n)).start()

    corr[me] = back_blocks[me]

    def returned(s):
        return remote(back_blocks.at[s], corr.at[s], back_send.at[s], back_recv.at[s], s)

    def finish(t):
        solve(t, 0, 2 * t)
        solve(t, blocks - 1, 2 * t + 1)
        pltpu.make_async_copy(adv.at[t], o_hbm.at[t], out_sem.at[t]).start()

    returned(twin).wait_recv()
    finish(my_pair)

    @pl.loop(1, tracers)
    def _(i):
        t = lax.rem(my_pair + tracers - i, tracers)
        returned(2 * t).wait_recv()
        returned(2 * t + 1).wait_recv()
        finish(t)

    for halo in halos:
        halo.wait_send()

    @pl.loop(1, n)
    def _(k):
        dest = lax.rem(me + k, n)
        send(dest).wait_send()
        back(dest).wait_send()

    @pl.loop(0, tracers)
    def _(t):
        pltpu.make_async_copy(adv.at[t], o_hbm.at[t], out_sem.at[t]).wait()


def flat_rows(x):
    count, levels, lons, lat_rows = x.shape
    x = x.transpose(0, 2, 1, 3).reshape(count, lons, levels, lat_rows // LANES, LANES)
    x = with_layout_constraint(x, Layout((0, 1, 3, 2, 4)))
    return x.transpose(0, 1, 3, 2, 4).reshape(count, lons * lat_rows // LANES * levels, LANES)


def local_by_kernel(n, tracer_field, courant_lon, courant_lat, diffusivity, polar_mask, cutoff):
    tracers, levels, lons, lat_rows = tracer_field.shape
    blocks = lat_rows // LANES
    rows = lons * blocks * levels
    field = flat_rows(tracer_field)
    speeds = [flat_rows(x[None])[0] for x in (courant_lon, courant_lat)]
    length = n * lons
    g = orthonormal_rows(length).astype(np.float32)
    tables = []
    for x in (g, g.T):
        high = x.astype(jnp.bfloat16)
        tables += [high, (x - high.astype(np.float32)).astype(jnp.bfloat16)]
    f32 = jnp.float32
    result = pl.pallas_call(
        functools.partial(kernel, n, tracers, lons, blocks),
        out_shape=jax.ShapeDtypeStruct((tracers, rows, LANES), f32),
        in_specs=[pl.BlockSpec(memory_space=pl.ANY)] * 7,
        out_specs=pl.BlockSpec(memory_space=pl.ANY),
        scratch_shapes=[
            pltpu.VMEM((tracers + 1, rows + 32, LANES), f32),
            pltpu.VMEM((rows + 8, LANES), f32),
            pltpu.VMEM((lons * blocks, LANES), f32),
            pltpu.VMEM((lat_rows,), jnp.int32),
            pltpu.VMEM((lat_rows,), jnp.int32),
            pltpu.VMEM((4, length, length), jnp.bfloat16),
            pltpu.VMEM((5, rows, LANES), f32),
            pltpu.VMEM((tracers, rows, LANES), f32),
            pltpu.VMEM((n, 2 * lons, LANES), f32),
            pltpu.VMEM((n, 2 * lons, LANES), f32),
            pltpu.VMEM((length, 2 * LANES), f32),
            pltpu.VMEM((n, 2 * lons, LANES), f32),
            pltpu.VMEM((n, 2 * lons, LANES), f32),
            pltpu.SemaphoreType.DMA((7,)),
            pltpu.SemaphoreType.DMA((3,)),
            pltpu.SemaphoreType.DMA((3,)),
            pltpu.SemaphoreType.DMA((n,)),
            pltpu.SemaphoreType.DMA((n,)),
            pltpu.SemaphoreType.DMA((n,)),
            pltpu.SemaphoreType.DMA((n,)),
            pltpu.SemaphoreType.DMA((tracers,)),
        ],
        compiler_params=pltpu.CompilerParams(collective_id=0, has_side_effects=True),
    )(
        field,
        *speeds,
        diffusivity.reshape(lons * blocks, LANES),
        cutoff,
        polar_mask,
        jnp.asarray(np.stack(tables)),
    )
    result = result.reshape(tracers, lons, blocks, levels, LANES).transpose(0, 1, 3, 2, 4)
    return result.reshape(tracers, lons, levels, lat_rows).transpose(0, 2, 1, 3)


def solution(mesh):
    n = mesh.shape["lon"]
    members = mesh.shape["member"]
    placed = (
        P("member", None, "lon", None),
        P("member", "lon", None),
        P("member", "lon", None),
        P("member", "lon", None),
        P(),
        P(),
    )

    def run(tracer_field, *rest):
        tracers, levels, length, lat_rows = tracer_field.shape
        fits = (
            n == 2 * (tracers // members)
            and levels == 2
            and lat_rows % LANES == 0
            and (length // n) * (lat_rows // LANES) % 4 == 0
            and lat_rows // LANES <= 8
        )
        local = functools.partial(local_by_kernel, n) if fits else local_by_collectives
        return jax.shard_map(
            local, mesh=mesh, in_specs=placed, out_specs=P("member", None, "lon", None), check_vma=False
        )(tracer_field, *rest)

    return run
```

time: 90 us -> 24.8 us (0.28)
  waiting for transfers between devices: 30 us -> 0 us
  local copies, waits for them, and re-layouts: 31.3 us -> 1.94 us
  Pallas kernels: 0 us -> 22.7 us
  starting transfers between devices: 15 us -> 0 us
  other arithmetic: 8.27 us -> 0 us
  matrix products: 4.66 us -> 0 us
    all_to_all x2 -> x0, waiting for transfers between devices: 30 us -> none  [the longest x1 15.4 us: local(): lax.all_to_all(removed, 'lon', split_axis=1, concat_axis=2, tiled=True)]
    pallas_call x0 -> x1, Pallas kernels: none -> 22.7 us  [local_by_kernel(): pl.pallas_call(functools.partial(kernel, n, tracers, lons, blocks), out_s...]
    unnamed x21 -> x1, local copies, waits for them, and re-layouts: 13.4 us -> 1.94 us
    all_to_all x2 -> x0, starting transfers between devices: 9.4 us -> none  [the longest x1 4.97 us: local(): lax.all_to_all(batched, 'lon', split_axis=2, concat_axis=1, tiled=True)]
    all_to_all x5 -> x0, local copies, waits for them, and re-layouts: 8.17 us -> none  [the longest x3 5.92 us: local(): lax.all_to_all(batched, 'lon', split_axis=2, concat_axis=1, tiled=True)]
    ppermute x2 -> x0, starting transfers between devices: 5.56 us -> none  [the longest x1 5.06 us: padded(): after = lax.ppermute(leading, axis, down)]
    reshape x2 -> x0, local copies, waits for them, and re-layouts: 5.38 us -> none  [local(): batched = advected.reshape(tracers * levels, lon_local, lat_rows)]
    dot_general x4 -> x0, matrix products: 4.66 us -> none  [the longest x1 1.18 us: high_part(): jnp.einsum('brm,im->bir', imag_part * keeper[None], sine, precision=highest)]
  transfers between devices with their start and end apart: 4 -> 0, of which waited for: 2 -> 0; matrix products, arithmetic and copies ran while one was open for 4% -> 0% of each run, Pallas kernels for 0% -> 0%
where the time goes in v1:
time: 24.8 us; the launch traced here: 24.7 us
  Pallas kernels  22.7 us (92%)
  local copies, waits for them, and re-layouts  1.94 us (8%)
    pallas_call x1, Pallas kernels, local_by_kernel(): pl.pallas_call(functools.partial(kernel, n, tracers, lons, blocks), out_s...  22.7 us
    unnamed x1, local copies, waits for them, and re-layouts  1.94 us

profile of v1, /device:TPU:0, one launch (start us, length us, event | category | flops | bytes accessed | tf_op | source)
XLA Modules:
  0.0 24.7 jit_solution(3307435457154067893)
XLA Ops:
  0.0 22.7 %shard_map.73 = f32[8,144,128]{2,1,0:T(8,128)} custom-call(f32[8,144,128]{2,1,0:T(8,128)} %bitcast.34, f32[144,128]{1,0:T(8,128)} %bitcast.35, f32[144,128]{1,0:T(8,128)} %bitcast.36, f32[72,128]{1,0:T(8,128)} %bitcast.37, s32[768]{0:T(1024)} %cut_hbm.1, s32[768]{0:T(1024)} %mask_hbm.1, bf16[4,192,192]{2,1,0:T(8,128)(2,1)} %constant.2.clone.g_hbm), custom_call_target="tpu_custom_call" | custom-call | tf_op jit(solution)/shard_map/pallas_call | solution.py:331
  22.7 1.9 %copy.9 = f32[8,2,12,768]{3,1,2,0:T(2,128)} copy(f32[8,2,12,768]{3,1,2,0:T(2,128)} %bitcast.33) | data formatting | bytes 1179648

commit v2 on v1

--- a/solution.py
+++ b/solution.py
@@ -122,13 +122,14 @@
 
 def kernel(
     n, tracers, lons, blocks,
-    t_hbm, c_hbm, cl_hbm, kd_hbm, cut_hbm, mask_hbm, g_hbm, o_hbm,
-    buf, clv, kv, cutv, maskv, gv, coef, adv, out_blocks, in_blocks, spec, back_blocks, corr,
+    t_hbm, c_hbm, cl_hbm, kd_hbm, cut_hbm, mask_hbm, g_hbm, gt_hbm, o_hbm,
+    buf, clv, kv, cutv, maskv, gv, gtv, coef, adv, out_blocks, in_blocks, spec, back_blocks, corr,
     in_sem, halo_send, halo_recv, send_sem, recv_sem, back_send, back_recv, out_sem,
 ):
     rows = lons * blocks * 2
     stride = blocks * 2
     top = 16
+    slot = spec.shape[0] // n
     me = lax.axis_index("lon")
     right, left = lax.rem(me + 1, n), lax.rem(me + n - 1, n)
     my_pair = me // 2
@@ -142,6 +143,7 @@
         pltpu.make_async_copy(cut_hbm, cutv, in_sem.at[4]),
         pltpu.make_async_copy(mask_hbm, maskv, in_sem.at[5]),
         pltpu.make_async_copy(g_hbm, gv, in_sem.at[6]),
+        pltpu.make_async_copy(gt_hbm, gtv, in_sem.at[7]),
     ]
     for load in loads:
         load.start()
@@ -168,6 +170,7 @@
     for halo in halos:
         halo.start()
 
+    spec[...] = jnp.zeros_like(spec)
     clv[pl.ds(0, 8)] = jnp.zeros((8, LANES), jnp.float32)
     loads[1].wait()
     row = lax.rem(lax.broadcasted_iota(jnp.int32, (rows, LANES), 0), stride)
@@ -208,9 +211,13 @@
                 first = h * (stride - 2) + lev
                 out_blocks[2 * t + h, pl.ds(lev * lons, lons)] = adv[t, pl.ds(first, lons, stride=stride)]
 
-    @pl.loop(1, tracers)
+    def pair_at(i):
+        offset = tracers // 2 + (1 - 2 * lax.rem(i, 2)) * ((i + 1) // 2)
+        return lax.rem(my_pair + offset, tracers)
+
+    @pl.loop(0, tracers - 1)
     def _(i):
-        t = lax.rem(my_pair + i, tracers)
+        t = pair_at(i)
         advect(t)
         send(2 * t).start()
         send(2 * t + 1).start()
@@ -246,13 +253,10 @@
     def received(s):
         return remote(out_blocks.at[s], in_blocks.at[s], send_sem.at[s], recv_sem.at[s], s)
 
-    @pl.loop(1, n)
-    def _(k):
-        received(lax.rem(me + n - k, n)).wait_recv()
-
-    for s in range(n):
+    def pack(s):
+        first = pl.multiple_of(s * slot, slot)
         for lev in range(2):
-            spec[pl.ds(s * lons, lons), pl.ds(lev * LANES, LANES)] = in_blocks[s, pl.ds(lev * lons, lons)]
+            spec[pl.ds(first, lons), pl.ds(lev * LANES, LANES)] = in_blocks[s, pl.ds(lev * lons, lons)]
 
     length = n * lons
     cut = jnp.where(half == 0, cutv[pl.ds(0, LANES)], cutv[pl.ds((blocks - 1) * LANES, LANES)])
@@ -260,19 +264,38 @@
     cut = jnp.where(mask == 1, cut, length).reshape(1, LANES)
     wave = lax.rem(lax.broadcasted_iota(jnp.int32, (length, LANES), 0), length // 2) + 1
     keep = wave > cut
+    pack(me)
+    received(twin).wait_recv()
+    pack(twin)
+
+    @pl.loop(0, tracers - 1)
+    def _(i):
+        pair = pair_at(tracers - 2 - i)
+        for h in range(2):
+            received(2 * pair + h).wait_recv()
+            pack(2 * pair + h)
+
     waves = product(gv[0], gv[1], spec[...])
     waves = jnp.where(jnp.concatenate([keep, keep], axis=1), waves, 0.0)
-    spec[...] = product(gv[2], gv[3], waves)
-    for s in range(n):
+    spec[...] = product(gtv[0], gtv[1], waves)
+    def unpack(s):
+        first = pl.multiple_of(s * slot, slot)
         for lev in range(2):
-            back_blocks[s, pl.ds(lev * lons, lons)] = spec[pl.ds(s * lons, lons), pl.ds(lev * LANES, LANES)]
+            back_blocks[s, pl.ds(lev * lons, lons)] = spec[pl.ds(first, lons), pl.ds(lev * LANES, LANES)]
 
     def back(dest):
         return remote(back_blocks.at[dest], corr.at[me], back_send.at[dest], back_recv.at[me], dest)
 
-    @pl.loop(1, n)
-    def _(k):
-        back(lax.rem(me + k, n)).start()
+    @pl.loop(0, tracers - 1)
+    def _(i):
+        pair = pair_at(i)
+        for h in range(2):
+            unpack(2 * pair + h)
+            back(2 * pair + h).start()
+
+    unpack(twin)
+    back(twin).start()
+    unpack(me)
 
     corr[me] = back_blocks[me]
 
@@ -287,9 +310,9 @@
     returned(twin).wait_recv()
     finish(my_pair)
 
-    @pl.loop(1, tracers)
+    @pl.loop(0, tracers - 1)
     def _(i):
-        t = lax.rem(my_pair + tracers - i, tracers)
+        t = pair_at(tracers - 2 - i)
         returned(2 * t).wait_recv()
         returned(2 * t + 1).wait_recv()
         finish(t)
@@ -323,15 +346,17 @@
     speeds = [flat_rows(x[None])[0] for x in (courant_lon, courant_lat)]
     length = n * lons
     g = orthonormal_rows(length).astype(np.float32)
-    tables = []
-    for x in (g, g.T):
-        high = x.astype(jnp.bfloat16)
-        tables += [high, (x - high.astype(np.float32)).astype(jnp.bfloat16)]
+    slot = -(-lons // 8) * 8
+    wide = np.zeros((length, n, slot), np.float32)
+    wide[:, :, :lons] = g.reshape(length, n, lons)
+    wide = wide.reshape(length, n * slot)
+    high = wide.astype(jnp.bfloat16)
+    table = np.stack([high, (wide - high.astype(np.float32)).astype(jnp.bfloat16)])
     f32 = jnp.float32
     result = pl.pallas_call(
         functools.partial(kernel, n, tracers, lons, blocks),
         out_shape=jax.ShapeDtypeStruct((tracers, rows, LANES), f32),
-        in_specs=[pl.BlockSpec(memory_space=pl.ANY)] * 7,
+        in_specs=[pl.BlockSpec(memory_space=pl.ANY)] * 8,
         out_specs=pl.BlockSpec(memory_space=pl.ANY),
         scratch_shapes=[
             pltpu.VMEM((tracers + 1, rows + 32, LANES), f32),
@@ -339,15 +364,16 @@
             pltpu.VMEM((lons * blocks, LANES), f32),
             pltpu.VMEM((lat_rows,), jnp.int32),
             pltpu.VMEM((lat_rows,), jnp.int32),
-            pltpu.VMEM((4, length, length), jnp.bfloat16),
+            pltpu.VMEM((2, length, n * slot), jnp.bfloat16),
+            pltpu.VMEM((2, n * slot, length), jnp.bfloat16),
             pltpu.VMEM((5, rows, LANES), f32),
             pltpu.VMEM((tracers, rows, LANES), f32),
             pltpu.VMEM((n, 2 * lons, LANES), f32),
             pltpu.VMEM((n, 2 * lons, LANES), f32),
-            pltpu.VMEM((length, 2 * LANES), f32),
+            pltpu.VMEM((n * slot, 2 * LANES), f32),
             pltpu.VMEM((n, 2 * lons, LANES), f32),
             pltpu.VMEM((n, 2 * lons, LANES), f32),
-            pltpu.SemaphoreType.DMA((7,)),
+            pltpu.SemaphoreType.DMA((8,)),
             pltpu.SemaphoreType.DMA((3,)),
             pltpu.SemaphoreType.DMA((3,)),
             pltpu.SemaphoreType.DMA((n,)),
@@ -363,7 +389,8 @@
         diffusivity.reshape(lons * blocks, LANES),
         cutoff,
         polar_mask,
-        jnp.asarray(np.stack(tables)),
+        jnp.asarray(table),
+        jnp.asarray(np.ascontiguousarray(table.transpose(0, 2, 1))),
     )
     result = result.reshape(tracers, lons, blocks, levels, LANES).transpose(0, 1, 3, 2, 4)
     return result.reshape(tracers, lons, levels, lat_rows).transpose(0, 2, 1, 3)

time: 24.8 us -> 26.5 us (1.069)
  Pallas kernels: 22.7 us -> 24.4 us
    pallas_call x1, Pallas kernels: 22.7 us -> 24.4 us  [local_by_kernel(): pl.pallas_call(functools.partial(kernel, n, tracers, lons, blocks), out_s...]
where the time goes in v2:
time: 26.5 us; the launch traced here: 26.4 us
  Pallas kernels  24.4 us (92%)
  local copies, waits for them, and re-layouts  1.94 us (7%)
    pallas_call x1, Pallas kernels, local_by_kernel(): pl.pallas_call(functools.partial(kernel, n, tracers, lons, blocks), out_s...  24.4 us
    unnamed x1, local copies, waits for them, and re-layouts  1.94 us

profile of v2, /device:TPU:0, one launch (start us, length us, event | category | flops | bytes accessed | tf_op | source)
XLA Modules:
  0.0 26.4 jit_solution(14029616945344061197)
XLA Ops:
  0.0 24.4 %shard_map.82 = f32[8,144,128]{2,1,0:T(8,128)} custom-call(f32[8,144,128]{2,1,0:T(8,128)} %bitcast.34, f32[144,128]{1,0:T(8,128)} %bitcast.35, f32[144,128]{1,0:T(8,128)} %bitcast.36, f32[72,128]{1,0:T(8,128)} %bitcast.37, s32[768]{0:T(1024)} %cut_hbm.1, s32[768]{0:T(1024)} %mask_hbm.1, bf16[2,192,256]{2,1,0:T(8,128)(2,1)} %constant.4.clone.g_hbm, ...), custom_call_target="tpu_custom_call" | custom-call | tf_op jit(solution)/shard_map/pallas_call | solution.py:356
  24.5 1.9 %copy.10 = f32[8,2,12,768]{3,1,2,0:T(2,128)} copy(f32[8,2,12,768]{3,1,2,0:T(2,128)} %bitcast.33) | data formatting | bytes 1179648

commit v3 on v2

--- a/solution.py
+++ b/solution.py
@@ -172,59 +172,96 @@
 
     spec[...] = jnp.zeros_like(spec)
     clv[pl.ds(0, 8)] = jnp.zeros((8, LANES), jnp.float32)
-    loads[1].wait()
-    row = lax.rem(lax.broadcasted_iota(jnp.int32, (rows, LANES), 0), stride)
-    lane = lax.broadcasted_iota(jnp.int32, (rows, LANES), 1)
-    last_lane, first_lane = lane == LANES - 1, lane == 0
-    cl = clv[pl.ds(8, rows)]
-    cl_prev = pltpu.roll(jnp.where(last_lane, clv[pl.ds(6, rows)], cl), 1, axis=1)
-    cl_prev = jnp.where((row < 2) & first_lane, 0.0, cl_prev)
-    north_next = jnp.where((row >= stride - 2) & last_lane, 0.0, jnp.minimum(cl, 0.0))
-    coef[3] = -north_next
-    coef[4] = jnp.maximum(cl_prev, 0.0)
-    rest = 1.0 - jnp.maximum(cl, 0.0) + jnp.minimum(cl_prev, 0.0)
-    loads[0].wait()
-    halos[0].wait_recv()
-    c = buf[tracers, pl.ds(top, rows)]
-    c_west = buf[tracers, pl.ds(top - stride, rows)]
-    coef[0] = rest - jnp.maximum(c, 0.0) + jnp.minimum(c_west, 0.0)
-    coef[1] = -jnp.minimum(c, 0.0)
-    coef[2] = jnp.maximum(c_west, 0.0)
-    loads[2].wait()
-    halos[1].wait_recv()
-    halos[2].wait_recv()
-
-    def send(dest):
-        return remote(out_blocks.at[dest], in_blocks.at[me], send_sem.at[dest], recv_sem.at[me], dest)
-
-    def advect(t):
-        x = buf[t, pl.ds(top, rows)]
-        y = jnp.where(first_lane, buf[t, pl.ds(top + 2, rows)], x)
-        total = coef[0] * x + coef[3] * pltpu.roll(y, LANES - 1, axis=1)
-        y = jnp.where(last_lane, buf[t, pl.ds(top - 2, rows)], x)
-        total += coef[4] * pltpu.roll(y, 1, axis=1)
-        total += coef[1] * buf[t, pl.ds(top + stride, rows)]
-        total += coef[2] * buf[t, pl.ds(top - stride, rows)]
-        adv[t] = total
+    def factors(start, count):
+        row = lax.rem(lax.broadcasted_iota(jnp.int32, (count, LANES), 0), stride)
+        lane = lax.broadcasted_iota(jnp.int32, (count, LANES), 1)
+        last_lane, first_lane = lane == LANES - 1, lane == 0
+        here = pl.ds(start, count)
+        cl = clv[pl.ds(8 + start, count)]
+        cl_prev = pltpu.roll(jnp.where(last_lane, clv[pl.ds(6 + start, count)], cl), 1, axis=1)
+        cl_prev = jnp.where((row < 2) & first_lane, 0.0, cl_prev)
+        north_next = jnp.where((row >= stride - 2) & last_lane, 0.0, jnp.minimum(cl, 0.0))
+        c = buf[tracers, pl.ds(top + start, count)]
+        c_west = buf[tracers, pl.ds(top + start - stride, count)]
+        rest = 1.0 - jnp.maximum(cl, 0.0) + jnp.minimum(cl_prev, 0.0)
+        coef[0, here] = rest - jnp.maximum(c, 0.0) + jnp.minimum(c_west, 0.0)
+        coef[1, here] = -jnp.minimum(c, 0.0)
+        coef[2, here] = jnp.maximum(c_west, 0.0)
+        coef[3, here] = -north_next
+        coef[4, here] = jnp.maximum(cl_prev, 0.0)
+
+    def advect(t, start, count):
+        lane = lax.broadcasted_iota(jnp.int32, (count, LANES), 1)
+        here = pl.ds(start, count)
+        x = buf[t, pl.ds(top + start, count)]
+        y = jnp.where(lane == 0, buf[t, pl.ds(top + start + 2, count)], x)
+        total = coef[0, here] * x + coef[3, here] * pltpu.roll(y, LANES - 1, axis=1)
+        y = jnp.where(lane == LANES - 1, buf[t, pl.ds(top + start - 2, count)], x)
+        total += coef[4, here] * pltpu.roll(y, 1, axis=1)
+        total += coef[1, here] * buf[t, pl.ds(top + start + stride, count)]
+        total += coef[2, here] * buf[t, pl.ds(top + start - stride, count)]
+        adv[t, here] = total
+
+    early = 8
+    late = lons - early
+    cuts = ((0, stride), ((early + 1) * stride, (lons - early - 1) * stride))
+
+    def cut_early(t):
+        advect(t, stride, early * stride)
+        for h in range(2):
+            for lev in range(2):
+                first = stride + h * (stride - 2) + lev
+                out_blocks[2 * t + h, pl.ds(lev * early, early)] = adv[t, pl.ds(first, early, stride=stride)]
+
+    def cut_late(t):
+        for start, count in cuts:
+            advect(t, start, count)
         for h in range(2):
             for lev in range(2):
                 first = h * (stride - 2) + lev
-                out_blocks[2 * t + h, pl.ds(lev * lons, lons)] = adv[t, pl.ds(first, lons, stride=stride)]
+                to = 2 * early + lev * late
+                out_blocks[2 * t + h, pl.ds(to, late - 1)] = adv[t, pl.ds((early + 1) * stride + first, late - 1, stride=stride)]
+                out_blocks[2 * t + h, pl.ds(to + late - 1, 1)] = adv[t, pl.ds(first, 1)]
 
     def pair_at(i):
-        offset = tracers // 2 + (1 - 2 * lax.rem(i, 2)) * ((i + 1) // 2)
-        return lax.rem(my_pair + offset, tracers)
+        return lax.rem(my_pair + i + 1, tracers)
+
+    parts = (pl.ds(0, 2 * early), pl.ds(2 * early, 2 * late))
+
+    def send(dest, part):
+        return remote(
+            out_blocks.at[dest, parts[part]], in_blocks.at[me, parts[part]],
+            send_sem.at[part, dest], recv_sem.at[part, me], dest,
+        )
+
+    twin = 2 * my_pair + 1 - half
+    for load in loads[:3]:
+        load.wait()
+    factors(stride, early * stride)
 
     @pl.loop(0, tracers - 1)
     def _(i):
         t = pair_at(i)
-        advect(t)
-        send(2 * t).start()
-        send(2 * t + 1).start()
-
-    advect(my_pair)
-    twin = 2 * my_pair + 1 - half
-    send(twin).start()
+        cut_early(t)
+        send(2 * t, 0).start()
+        send(2 * t + 1, 0).start()
+
+    cut_early(my_pair)
+    send(twin, 0).start()
+    for halo in halos:
+        halo.wait_recv()
+    for start, count in cuts:
+        factors(start, count)
+
+    @pl.loop(0, tracers - 1)
+    def _(i):
+        t = pair_at(i)
+        cut_late(t)
+        send(2 * t, 1).start()
+        send(2 * t + 1, 1).start()
+
+    cut_late(my_pair)
+    send(twin, 1).start()
     in_blocks[me] = out_blocks[me]
 
     loads[3].wait()
@@ -250,13 +287,19 @@
     for load in loads[4:]:
         load.wait()
 
-    def received(s):
-        return remote(out_blocks.at[s], in_blocks.at[s], send_sem.at[s], recv_sem.at[s], s)
+    def receive(s):
+        for part in range(2):
+            remote(
+                out_blocks.at[s, parts[part]], in_blocks.at[s, parts[part]],
+                send_sem.at[part, s], recv_sem.at[part, s], s,
+            ).wait_recv()
 
     def pack(s):
         first = pl.multiple_of(s * slot, slot)
         for lev in range(2):
-            spec[pl.ds(first, lons), pl.ds(lev * LANES, LANES)] = in_blocks[s, pl.ds(lev * lons, lons)]
+            lanes = pl.ds(lev * LANES, LANES)
+            spec[pl.ds(first, early), lanes] = in_blocks[s, pl.ds(lev * early, early)]
+            spec[pl.ds(first + early, late), lanes] = in_blocks[s, pl.ds(2 * early + lev * late, late)]
 
     length = n * lons
     cut = jnp.where(half == 0, cutv[pl.ds(0, LANES)], cutv[pl.ds((blocks - 1) * LANES, LANES)])
@@ -265,14 +308,14 @@
     wave = lax.rem(lax.broadcasted_iota(jnp.int32, (length, LANES), 0), length // 2) + 1
     keep = wave > cut
     pack(me)
-    received(twin).wait_recv()
+    receive(twin)
     pack(twin)
 
     @pl.loop(0, tracers - 1)
     def _(i):
         pair = pair_at(tracers - 2 - i)
         for h in range(2):
-            received(2 * pair + h).wait_recv()
+            receive(2 * pair + h)
             pack(2 * pair + h)
 
     waves = product(gv[0], gv[1], spec[...])
@@ -323,7 +366,8 @@
     @pl.loop(1, n)
     def _(k):
         dest = lax.rem(me + k, n)
-        send(dest).wait_send()
+        send(dest, 0).wait_send()
+        send(dest, 1).wait_send()
         back(dest).wait_send()
 
     @pl.loop(0, tracers)
@@ -347,11 +391,13 @@
     length = n * lons
     g = orthonormal_rows(length).astype(np.float32)
     slot = -(-lons // 8) * 8
-    wide = np.zeros((length, n, slot), np.float32)
-    wide[:, :, :lons] = g.reshape(length, n, lons)
-    wide = wide.reshape(length, n * slot)
-    high = wide.astype(jnp.bfloat16)
-    table = np.stack([high, (wide - high.astype(np.float32)).astype(jnp.bfloat16)])
+    tables = []
+    for order in ([*range(1, lons), 0], [*range(lons)]):
+        wide = np.zeros((length, n, slot), np.float32)
+        wide[:, :, :lons] = g.reshape(length, n, lons)[:, :, order]
+        wide = wide.reshape(length, n * slot)
+        high = wide.astype(jnp.bfloat16)
+        tables.append(np.stack([high, (wide - high.astype(np.float32)).astype(jnp.bfloat16)]))
     f32 = jnp.float32
     result = pl.pallas_call(
         functools.partial(kernel, n, tracers, lons, blocks),
@@ -376,8 +422,8 @@
             pltpu.SemaphoreType.DMA((8,)),
             pltpu.SemaphoreType.DMA((3,)),
             pltpu.SemaphoreType.DMA((3,)),
-            pltpu.SemaphoreType.DMA((n,)),
-            pltpu.SemaphoreType.DMA((n,)),
+            pltpu.SemaphoreType.DMA((2, n)),
+            pltpu.SemaphoreType.DMA((2, n)),
             pltpu.SemaphoreType.DMA((n,)),
             pltpu.SemaphoreType.DMA((n,)),
             pltpu.SemaphoreType.DMA((tracers,)),
@@ -389,8 +435,8 @@
         diffusivity.reshape(lons * blocks, LANES),
         cutoff,
         polar_mask,
-        jnp.asarray(table),
-        jnp.asarray(np.ascontiguousarray(table.transpose(0, 2, 1))),
+        jnp.asarray(tables[0]),
+        jnp.asarray(np.ascontiguousarray(tables[1].transpose(0, 2, 1))),
     )
     result = result.reshape(tracers, lons, blocks, levels, LANES).transpose(0, 1, 3, 2, 4)
     return result.reshape(tracers, lons, levels, lat_rows).transpose(0, 2, 1, 3)
@@ -414,7 +460,7 @@
             n == 2 * (tracers // members)
             and levels == 2
             and lat_rows % LANES == 0
-            and (length // n) * (lat_rows // LANES) % 4 == 0
+            and length == 12 * n
             and lat_rows // LANES <= 8
         )
         local = functools.partial(local_by_kernel, n) if fits else local_by_collectives

time: 26.5 us -> 23.6 us (0.89)
  Pallas kernels: 24.4 us -> 21.3 us
    pallas_call x1, Pallas kernels: 24.4 us -> 21.3 us  [local_by_kernel(): pl.pallas_call(functools.partial(kernel, n, tracers, lons, blocks), out_s...]
where the time goes in v3:
time: 23.6 us; the launch traced here: 23.3 us
  Pallas kernels  21.3 us (90%)
  local copies, waits for them, and re-layouts  1.94 us (8%)
    pallas_call x1, Pallas kernels, local_by_kernel(): pl.pallas_call(functools.partial(kernel, n, tracers, lons, blocks), out_s...  21.3 us
    unnamed x1, local copies, waits for them, and re-layouts  1.94 us

profile of v3, /device:TPU:0, one launch (start us, length us, event | category | flops | bytes accessed | tf_op | source)
XLA Modules:
  0.0 23.3 jit_solution(10437030502809112680)
XLA Ops:
  0.0 21.3 %shard_map.82 = f32[8,144,128]{2,1,0:T(8,128)} custom-call(f32[8,144,128]{2,1,0:T(8,128)} %bitcast.34, f32[144,128]{1,0:T(8,128)} %bitcast.35, f32[144,128]{1,0:T(8,128)} %bitcast.36, f32[72,128]{1,0:T(8,128)} %bitcast.37, s32[768]{0:T(1024)} %cut_hbm.1, s32[768]{0:T(1024)} %mask_hbm.1, bf16[2,192,256]{2,1,0:T(8,128)(2,1)} %constant.4.clone.g_hbm, ...), custom_call_target="tpu_custom_call" | custom-call | tf_op jit(solution)/shard_map/pallas_call | solution.py:402
  21.3 1.9 %copy.10 = f32[8,2,12,768]{3,1,2,0:T(2,128)} copy(f32[8,2,12,768]{3,1,2,0:T(2,128)} %bitcast.33) | data formatting | bytes 1179648

commit v4 on v3

--- a/solution.py
+++ b/solution.py
@@ -154,8 +154,6 @@
     def _(k):
         pl.semaphore_signal(barrier, inc=1, device_id={"lon": lax.rem(me + k, n)}, device_id_type=pl.DeviceIdType.MESH)
 
-    pl.semaphore_wait(barrier, n - 1)
-
     def remote(src, dst, send, recv, to):
         return pltpu.make_async_remote_copy(
             src_ref=src, dst_ref=dst, send_sem=send, recv_sem=recv,
@@ -167,9 +165,6 @@
         remote(t_hbm.at[:, pl.ds(rows - 16, 16)], buf.at[pl.ds(0, tracers), pl.ds(0, 16)], halo_send.at[1], halo_recv.at[1], right),
         remote(t_hbm.at[:, pl.ds(0, 16)], buf.at[pl.ds(0, tracers), pl.ds(top + rows, 16)], halo_send.at[2], halo_recv.at[2], left),
     ]
-    for halo in halos:
-        halo.start()
-
     spec[...] = jnp.zeros_like(spec)
     clv[pl.ds(0, 8)] = jnp.zeros((8, LANES), jnp.float32)
     def factors(start, count):
@@ -239,14 +234,20 @@
         load.wait()
     factors(stride, early * stride)
 
+    @pl.loop(0, tracers)
+    def _(t):
+        cut_early(t)
+
+    pl.semaphore_wait(barrier, n - 1)
+    for halo in halos:
+        halo.start()
+
     @pl.loop(0, tracers - 1)
     def _(i):
         t = pair_at(i)
-        cut_early(t)
         send(2 * t, 0).start()
         send(2 * t + 1, 0).start()
 
-    cut_early(my_pair)
     send(twin, 0).start()
     for halo in halos:
         halo.wait_recv()

time: 23.6 us -> 23.9 us (1.013)
  Pallas kernels: 21.3 us -> 21.8 us
    pallas_call x1, Pallas kernels: 21.3 us -> 21.8 us  [local_by_kernel(): pl.pallas_call(functools.partial(kernel, n, tracers, lons, blocks), out_s...]
where the time goes in v4:
time: 23.9 us; the launch traced here: 23.8 us
  Pallas kernels  21.8 us (91%)
  local copies, waits for them, and re-layouts  1.94 us (8%)
    pallas_call x1, Pallas kernels, local_by_kernel(): pl.pallas_call(functools.partial(kernel, n, tracers, lons, blocks), out_s...  21.8 us
    unnamed x1, local copies, waits for them, and re-layouts  1.94 us

profile of v4, /device:TPU:0, one launch (start us, length us, event | category | flops | bytes accessed | tf_op | source)
XLA Modules:
  0.0 23.8 jit_solution(5077590722350211580)
XLA Ops:
  0.0 21.8 %shard_map.82 = f32[8,144,128]{2,1,0:T(8,128)} custom-call(f32[8,144,128]{2,1,0:T(8,128)} %bitcast.34, f32[144,128]{1,0:T(8,128)} %bitcast.35, f32[144,128]{1,0:T(8,128)} %bitcast.36, f32[72,128]{1,0:T(8,128)} %bitcast.37, s32[768]{0:T(1024)} %cut_hbm.1, s32[768]{0:T(1024)} %mask_hbm.1, bf16[2,192,256]{2,1,0:T(8,128)(2,1)} %constant.4.clone.g_hbm, ...), custom_call_target="tpu_custom_call" | custom-call | tf_op jit(solution)/shard_map/pallas_call | solution.py:403
  21.8 1.9 %copy.10 = f32[8,2,12,768]{3,1,2,0:T(2,128)} copy(f32[8,2,12,768]{3,1,2,0:T(2,128)} %bitcast.33) | data formatting | bytes 1179648
